TPU v7x, 32 devices: a whole 2x2x4 slice. The times are simulated.
32 devices in a mesh: ctx: 16 (over z, y, core), tp: 2 (over x).
Axes of the slice: x: 2, y: 2, z: 4, core: 2. Of those that a mesh axis runs over, the one named last changes fastest.
Arguments:
- hidden_in: bfloat16 [2048, 1536], P('ctx', 'tp'), may hold values from -60 to 60
- queries: bfloat16 [2048, 2048], P('ctx', 'tp'), may hold values from -200 to 200
- rotated_key_value: bfloat16 [2048, 4, 128], P('ctx', 'tp'), may hold values from -5 to 5
- sink_logit_table: float32 [32], P('tp'), may hold values from -2 to 2
- out_proj: bfloat16 [2048, 1536], P('tp', 'ctx'), may hold values from -0.125 to 0.125
- norm_gain: float32 [1536], P('tp'), may hold values from 0.1 to 1.9
- expert_in: bfloat16 [16, 2, 1536, 1536], P('ctx', None, None, 'tp'), may hold values from -0.15625 to 0.15625
- expert_out: bfloat16 [16, 1536, 1536], P('ctx', 'tp'), may hold values from -0.15625 to 0.15625
- routes: int32 [2048, 4], P('ctx'), may hold values from 0 to 15, all different within a row; in each aligned block of 128 rows (0 to 127, 128 to 255, ...) at most 96 rows name the same one
- route_scores: float32 [2048, 4], P('ctx'), may hold values from 0.05 to 1
Outputs:
- layer_out: bfloat16 [2048, 1536], P('ctx', 'tp')
Inputs may be any that keep to these rules, and one draw needn't show every extreme that they name: `routes`: each token names 4 different experts. In every aligned block of 128 tokens (the tokens of one device) no expert is named by more than 96 tokens, a bound that some block reaches.
All inputs are finite; a program needn't handle non-finite values.
Results may differ from a plain program's by a relative error of at most 0.008.
Values may be sent and summed in bfloat16 or wider, within the bound.
A program may use at most 64 MiB of HBM per device.

v0:
```python
import jax
import jax.numpy as jnp
from jax import lax
from jax.sharding import PartitionSpec as P

WINDOW_KEYS = 128


def shifted(value, axis, steps):
    count = lax.axis_size(axis)
    first, last = (max(0, -steps), min(count, count - steps))
    return lax.ppermute(value, axis, [(source, source + steps) for source in range(first, last)])


def attend(query_block, key_blk, value_blk, inside, sink_row_block, factor):
    score = (
        jnp.einsum("rgqd,sgd->gqrs", query_block, key_blk, preferred_element_type=jnp.float32)
        * factor
    )
    masked = jnp.where(inside, score, -1e30)
    top_score = jnp.maximum(jnp.max(masked, -1), sink_row_block[:, :, None])
    expvals = jnp.where(inside, jnp.exp(score - top_score[..., None]), 0.0)
    denominator = jnp.sum(expvals, -1) + jnp.exp(sink_row_block[:, :, None] - top_score)
    probs = (expvals / denominator[..., None]).astype(jnp.bfloat16)
    mixed = jnp.einsum("gqrs,sgd->rgqd", probs, value_blk, preferred_element_type=jnp.float32)
    return mixed.astype(jnp.bfloat16)


def body(
    hidden_in,
    queries,
    rotated_key_value,
    sink_logit_table,
    out_proj,
    norm_gain,
    expert_in,
    expert_out,
    routes,
    route_scores,
):
    tok_rows = hidden_in.shape[0]
    kv_heads = rotated_key_value.shape[1]
    head_dim = rotated_key_value.shape[2] // 2
    q_heads = sink_logit_table.shape[0]
    queries_per_group = q_heads // kv_heads
    factor = head_dim ** (-0.5)
    sink_row_block = sink_logit_table.reshape(kv_heads, queries_per_group)
    earlier = shifted(rotated_key_value, "ctx", 1)
    keys_all = jnp.concatenate([earlier, rotated_key_value], 0)
    first_pos = lax.axis_index("ctx") * tok_rows
    block_row_count = min(512, tok_rows)
    query_block = queries.reshape(block_row_count, kv_heads, queries_per_group, head_dim)
    query_pos = first_pos + 0 + jnp.arange(block_row_count, dtype=jnp.int32)[:, None]
    key_pos = (
        first_pos
        + 0
        - WINDOW_KEYS
        + jnp.arange(block_row_count + WINDOW_KEYS, dtype=jnp.int32)[None, :]
    )
    inside = (key_pos <= query_pos) & (key_pos > query_pos - WINDOW_KEYS) & (key_pos >= 0)
    mixed = attend(
        query_block,
        keys_all[..., :head_dim],
        keys_all[..., head_dim:],
        inside,
        sink_row_block,
        factor,
    )
    outputs = mixed.reshape(block_row_count, q_heads * head_dim)
    head_partial = jnp.dot(
        outputs,
        lax.all_gather(out_proj, "ctx", axis=1, tiled=True),
        preferred_element_type=jnp.float32,
    )
    d_model = head_partial.shape[1]
    residual = hidden_in.astype(jnp.float32) + lax.psum_scatter(
        head_partial.astype(jnp.bfloat16), "tp", scatter_dimension=1, tiled=True
    ).astype(jnp.float32)
    square_total = lax.psum(jnp.sum(residual * residual, -1), "tp")
    normed = (residual * lax.rsqrt(square_total[:, None] / d_model + 1e-05) * norm_gain).astype(
        jnp.bfloat16
    )
    ctx_count = lax.axis_size("ctx")
    tp_count = lax.axis_size("tp")
    top_count = routes.shape[1]
    experts = ctx_count * expert_in.shape[0]
    capacity = max(2, min(tok_rows, 3 * top_count * tok_rows // experts))
    quarter_w = d_model // tp_count
    onehot = (routes[:, :, None] == jnp.arange(experts, dtype=jnp.int32)).astype(jnp.int32)
    per_tok = jnp.sum(onehot, 1)
    before = jnp.cumsum(per_tok, axis=0) - per_tok
    slot_ids = jnp.sum(onehot * before[:, None, :], -1)
    flat_index = (routes * capacity + slot_ids).reshape(-1)
    weights = route_scores / jnp.sum(route_scores, -1, keepdims=True)
    full_data = lax.all_gather(normed, "tp", axis=1, tiled=True)
    row_width = full_data.shape[1]
    spread = jnp.broadcast_to(full_data[:, None, :], (tok_rows, top_count, row_width)).reshape(
        -1, row_width
    )
    outbox = jnp.zeros((experts * capacity, row_width), jnp.bfloat16).at[flat_index].set(spread)
    arrived = lax.all_to_all(
        outbox.reshape(ctx_count, 1, capacity, row_width),
        "ctx",
        split_axis=0,
        concat_axis=1,
        tiled=True,
    )
    leading = arrived.shape[:3]
    row_data = arrived.reshape(-1, d_model)
    gate_vals = jnp.dot(row_data, expert_in[0, 0], preferred_element_type=jnp.float32)
    up_vals = jnp.dot(row_data, expert_in[0, 1], preferred_element_type=jnp.float32)
    activated = ((up_vals + 1.0) * gate_vals * jax.nn.sigmoid(1.702 * gate_vals)).astype(
        jnp.bfloat16
    )
    partial_value = jnp.dot(activated, expert_out[0], preferred_element_type=jnp.float32).astype(
        jnp.bfloat16
    )
    result = partial_value.reshape(leading + (d_model,))
    returned = lax.all_to_all(result, "ctx", split_axis=1, concat_axis=0, tiled=True)
    picked = returned.reshape(-1, d_model)[flat_index].reshape(tok_rows, top_count, d_model)
    expert_result = lax.psum_scatter(
        picked.astype(jnp.float32).astype(jnp.bfloat16), "tp", scatter_dimension=2, tiled=True
    )
    moe_sum = jnp.zeros((tok_rows, quarter_w), jnp.float32)
    for member in range(top_count):
        moe_sum = moe_sum + weights[:, member : member + 1] * expert_result[:, member].astype(
            jnp.float32
        )
    return (residual + moe_sum).astype(jnp.bfloat16)


def solution(mesh):
    in_specs = (
        P("ctx", "tp"),
        P("ctx", "tp"),
        P("ctx", "tp", None),
        P("tp"),
        P("tp", "ctx"),
        P("tp"),
        P("ctx", None, None, "tp"),
        P("ctx", "tp", None),
        P("ctx", None),
        P("ctx", None),
    )
    out_specs = P("ctx", "tp")
    return jax.shard_map(body, mesh=mesh, in_specs=in_specs, out_specs=out_specs, check_vma=False)
```

profile of v0, /device:TPU:0, one launch (start us, length us, event | category | flops | bytes accessed | tf_op | source)
XLA Modules:
  0.0 388.7 jit_solution(4120775506760316176)
XLA Ops:
  6.5 0.0 copy-start
  6.5 0.0 all-gather.2.cloned.1.call-start
  6.5 0.7 all-gather.2.cloned.1.call-update
  7.3 0.0 reduce-scatter.3.cloned.1.call-start
  7.3 1.0 copy.31
  8.3 2.4 collective-permute-start
  10.7 0.1 and_and_fusion
  10.8 1.1 copy.33
  11.9 0.7 max.17
  12.7 0.0 collective-permute-done
  12.7 0.5 fusion.8
  13.2 0.1 broadcast_maximum_fusion
  13.2 0.4 fusion.11
  13.7 0.1 exponential_add_fusion
  13.8 0.6 convolution_convert_fusion.2
  14.4 0.0 copy-start.4
  14.4 43.1 %all-gather.2.cloned.1.call-done = bf16[1024,1536]{0,1:T(8,128)(2,1)} async-done(((bf16[1024,96]{0,1:T(8,128)(2,1)}), bf16[1024,1536]{0,1:T(8,128)(2,1)}) %all-gather.2.cloned.1.call-update) | async-done | bytes 3145744 | tf_op jit(solution)/shard_map/all_gather | solution.py:72
  57.6 3.9 convolution_convert_fusion.1
  61.4 0.0 reduce-scatter.3.cloned.1.call-update
  61.5 0.0 copy-done.4
  61.5 0.1 copy.35
  61.6 0.2 reduce_window_sum.11
  61.8 0.1 copy.37
  61.9 0.1 copy.38
  62.0 0.1 reshape.117
  62.1 11.4 %reduce-scatter.3.cloned.1.call-done = bf16[128,768]{1,0:T(8,128)(2,1)} async-done(((bf16[128,1536]{1,0:T(8,128)(2,1)}), bf16[128,768]{1,0:T(8,128)(2,1)}) %reduce-scatter.3.cloned.1.call-update) | async-done | bytes 196624 | tf_op jit(solution)/shard_map/reduce_scatter | solution.py:76
  73.5 0.0 copy-done.2
  73.5 1.1 multiply_reduce_fusion
  74.6 4.9 %psum.7 = f32[128]{0:T(128)S(1)} all-reduce(f32[128]{0:T(128)S(1)} %multiply_reduce_fusion), channel_id=1, replica_groups=mesh['ctx'=16,'tp'=2] {'tp'}, use_global_device_ids=true, to_apply=%region_8.9 | all-reduce | flops 128 | bytes 1024 | tf_op jit(solution)/shard_map/psum | solution.py:79
  79.5 0.0 copy-done.6
  79.5 1.0 multiply_convert_fusion.1
  80.6 6.3 %all_gather.7 = bf16[128,1536]{1,0:T(8,128)(2,1)S(1)} all-gather(bf16[128,768]{1,0:T(8,128)(2,1)S(1)} %multiply_convert_fusion.1), channel_id=1, replica_groups=mesh['ctx'=16,'tp'=2] {'tp'}, dimensions={1}, use_global_device_ids=true | all-gather | bytes 589824 | tf_op jit(solution)/shard_map/all_gather | solution.py:95
  86.9 1.6 broadcast_in_dim.20
  88.5 3.7 reshape.140
  92.2 6.8 %scatter_custom_fusion = bf16[1536,1536]{1,0:T(8,128)(2,1)} fusion(s32[512]{0:T(512)S(1)} %bitcast.87, bf16[512,1536]{1,0:T(8,128)(2,1)} %reshape.140, bf16[]{:T(256)} %constant.14.clone.1), kind=kCustom, calls=%fused_computation.11 | custom fusion | bytes 4719104 | tf_op jit(solution)/shard_map/scatter | solution.py:100
  99.0 109.1 %all_to_all.8 = bf16[16,1,96,1536]{3,2,1,0:T(8,128)(2,1)S(1)} all-to-all(bf16[16,1,96,1536]{3,2,1,0:T(8,128)(2,1)} %bitcast.81), channel_id=1, replica_groups=mesh['ctx'=16,'tp'=2] {'ctx'}, dimensions={0} | all-to-all | bytes 9437184 | tf_op jit(solution)/shard_map/all_to_all | solution.py:101
  208.1 2.2 copy-done.1
  210.3 7.1 %fusion.1 = f32[1536,768]{1,0:T(8,128)} fusion(bf16[1536,1536]{1,0:T(8,128)(2,1)S(1)} %bitcast.83, bf16[1,2,1536,768]{3,2,1,0:T(8,128)(2,1)} %param.16), kind=kOutput, calls=%fused_computation.6 | convolution fusion | flops 3623878656 | bytes 11796480 | tf_op jit(solution)/shard_map/dot_general | solution.py:110
  217.5 13.9 %convolution_convert_fusion = bf16[1536,1536]{1,0:T(8,128)(2,1)} fusion(bf16[1,768,1536]{2,1,0:T(8,128)(2,1)S(1)} %copy-done, f32[1536,768]{1,0:T(8,128)} %fusion.1, bf16[1536,1536]{1,0:T(8,128)(2,1)} %bitcast.84, bf16[1,2,1536,768]{3,2,1,0:T(8,128)(2,1)} %param.16), kind=kOutput, calls=%fused_computation.2 | convolution fusion | flops 7259553792 | bytes 18874368 | tf_op jit(solution)/shard_map/dot_general | solution.py:115
  231.3 5.4 %all-to-all-start.1 = ((bf16[1,16,96,1536]{3,2,0,1:T(8,128)(2,1)}), bf16[1,16,96,1536]{3,2,0,1:T(8,128)(2,1)}, u32[]{:S(2)}, u32[]{:S(2)}) async-start(bf16[1,16,96,1536]{3,2,0,1:T(8,128)(2,1)} %bitcast.82), calls=%async_computation.2 | async-start | bytes 9437184 | tf_op jit(solution)/shard_map/all_to_all | solution.py:119
  236.7 0.0 reduce-scatter.5.cloned.1.call-start
  236.8 86.7 %all-to-all-done.1 = bf16[1,16,96,1536]{3,2,0,1:T(8,128)(2,1)} async-done(((bf16[1,16,96,1536]{3,2,0,1:T(8,128)(2,1)}), bf16[1,16,96,1536]{3,2,0,1:T(8,128)(2,1)}, u32[]{:S(2)}, u32[]{:S(2)}) %all-to-all-start.1) | async-done | bytes 4718624 | tf_op jit(solution)/shard_map/all_to_all | solution.py:119
  323.5 7.4 %gather_fusion = bf16[512,1536]{1,0:T(8,128)(2,1)} fusion(bf16[1536,1536]{1,0:T(8,128)(2,1)} %bitcast.17, s32[1024]{0:T(1024)S(1)} %pad_clamp_fusion), kind=kCustom, calls=%fused_computation | custom fusion | bytes 3147776 | tf_op jit(solution)/shard_map/gather | solution.py:120
  330.9 3.9 reshape.123
  334.8 2.9 copy.40
  337.6 0.0 reduce-scatter.5.cloned.1.call-update
  337.7 42.3 %reduce-scatter.5.cloned.1.call-done = bf16[128,4,768]{2,0,1:T(8,128)(2,1)} async-done(((bf16[128,4,1536]{2,0,1:T(8,128)(2,1)}), bf16[128,4,768]{2,0,1:T(8,128)(2,1)}) %reduce-scatter.5.cloned.1.call-update) | async-done | bytes 786448 | tf_op jit(solution)/shard_map/reduce_scatter | solution.py:121
  380.0 2.2 fusion.16
  (21 shorter events, 0.1 us)
Async XLA Ops:
  6.5 210.9 %copy-start = (bf16[1,768,1536]{2,1,0:T(8,128)(2,1)S(1)}, bf16[1,768,1536]{2,1,0:T(8,128)(2,1)}, u32[]{:S(2)}) copy-start(bf16[1,768,1536]{2,1,0:T(8,128)(2,1)} %param.17) | copy-start | bytes 7077892
  6.5 51.0 %all-gather.2.cloned.1.call-start = ((), (), s32[]{:S(2)}) async-start(), calls=%async_computation.4 | async-start | bytes 3342336 | tf_op jit(solution)/shard_map/all_gather | solution.py:72
  7.3 66.3 %reduce-scatter.3.cloned.1.call-start = ((), (), s32[]{:S(2)}) async-start(), calls=%async_computation.5 | async-start | bytes 589824 | tf_op jit(solution)/shard_map/reduce_scatter | solution.py:76
  8.3 4.4 %collective-permute-start = (bf16[128,2,128]{0,2,1:T(8,128)(2,1)S(1)}, bf16[128,2,128]{0,2,1:T(8,128)(2,1)S(1)}, u32[]{:S(2)}, u32[]{:S(2)}) collective-permute-start(bf16[128,2,128]{0,2,1:T(8,128)(2,1)S(1)} %copy.31), channel_id=1, source_target_pairs={{0,2},{2,4},{4,6},{6,8},{8,10},{10,12},{12,14},{14,16},{16,18},{18... | collective-permute-start | bytes 196616 | tf_op jit(solution)/shard_map/ppermute | solution.py:12
  14.4 47.0 %copy-start.4 = (s32[128,4]{0,1:T(4,128)S(1)}, s32[128,4]{0,1:T(4,128)}, u32[]{:S(2)}) copy-start(s32[128,4]{0,1:T(4,128)} %param.18) | copy-start | bytes 6148
  57.6 16.0 %copy-start.2 = (bf16[128,768]{1,0:T(8,128)(2,1)S(1)}, bf16[128,768]{1,0:T(8,128)(2,1)}, u32[]{:S(2)}) copy-start(bf16[128,768]{1,0:T(8,128)(2,1)} %param.10) | copy-start | bytes 589828
  57.6 22.0 %copy-start.6 = (f32[768]{0:T(1024)S(1)}, f32[768]{0:T(1024)}, u32[]{:S(2)}) copy-start(f32[768]{0:T(1024)} %param.15) | copy-start | bytes 9220
  208.1 2.2 copy-start.1
  231.3 92.2 %all-to-all-start.1 = ((bf16[1,16,96,1536]{3,2,0,1:T(8,128)(2,1)}), bf16[1,16,96,1536]{3,2,0,1:T(8,128)(2,1)}, u32[]{:S(2)}, u32[]{:S(2)}) async-start(bf16[1,16,96,1536]{3,2,0,1:T(8,128)(2,1)} %bitcast.82), calls=%async_computation.2 | async-start | bytes 9437184 | tf_op jit(solution)/shard_map/all_to_all | solution.py:119
  236.7 143.3 %reduce-scatter.5.cloned.1.call-start = ((), (), s32[]{:S(2)}) async-start(), calls=%async_computation.6 | async-start | bytes 2359296 | tf_op jit(solution)/shard_map/reduce_scatter | solution.py:121
  334.8 2.9 copy-start.5
  334.8 45.3 %copy-start.3 = (bf16[128,768]{1,0:T(8,128)(2,1)S(1)}, bf16[128,768]{1,0:T(8,128)(2,1)}, u32[]{:S(2)}) copy-start(bf16[128,768]{1,0:T(8,128)(2,1)} %reduce-scatter.3.cloned.1.call-done) | copy-start | bytes 589828
Sparse Core Ops, SparseCore 0:
  9.6 47.8 all-gather.1
  61.6 11.9 reduce-scatter.2
  337.8 42.1 reduce-scatter.4
where the time goes:
time: 389 us
  waiting for transfers between devices  184 us (47%)
  blocking collectives  120 us (31%)
  local copies, waits for them, and re-layouts  31.6 us (8%)
  matrix products  26 us (7%)
  between operations  13.3 us (3%)
  starting transfers between devices  7.82 us (2%)
  other arithmetic  5.29 us (1%)
    all_to_all x1, blocking collectives, body(): lax.all_to_all(outbox.reshape(ctx_count, 1, capacity, row_width), 'ctx',...  109 us
    all_to_all x1, waiting for transfers between devices, body(): lax.all_to_all(result, 'ctx', split_axis=1, concat_axis=0, tiled=True)  86.7 us
    all_gather x1, waiting for transfers between devices, body(): lax.all_gather(out_proj, 'ctx', axis=1, tiled=True)  43.1 us
    reduce_scatter x1, waiting for transfers between devices, body(): lax.psum_scatter(picked.astype(jnp.float32).astype(jnp.bfloat16), 'tp', s...  42.3 us
    dot_general x1, matrix products, body(): jnp.dot(activated, expert_out[0], preferred_element_type=jnp.float32)  13.9 us
    reduce_scatter x1, waiting for transfers between devices, body(): lax.psum_scatter(head_partial.astype(jnp.bfloat16), 'tp', scatter_dimensi...  11.4 us
  transfers between devices with their start and end apart: 5, of which 4 were waited for; matrix products, arithmetic and copies ran while one was open for 1% of the time, Pallas kernels for 0%

commit v1 on v0

--- a/solution.py
+++ b/solution.py
@@ -24,6 +24,26 @@
     probs = (expvals / denominator[..., None]).astype(jnp.bfloat16)
     mixed = jnp.einsum("gqrs,sgd->rgqd", probs, value_blk, preferred_element_type=jnp.float32)
     return mixed.astype(jnp.bfloat16)
+
+
+def dense_experts(residual, normed, expert_in, expert_out, routes, weights):
+    experts = lax.axis_size("ctx")
+    chosen = routes[:, :, None] == jnp.arange(experts, dtype=jnp.int32)
+    spread = jnp.sum(jnp.where(chosen, weights[:, :, None], 0.0), 1)
+    every = lax.all_gather(spread, "ctx", axis=0, tiled=True)
+    mine = lax.dynamic_slice_in_dim(every, lax.axis_index("ctx"), 1, 1)
+    wide = lax.all_gather(normed, "tp", axis=1, tiled=True)
+    row_data = lax.all_gather(wide, "ctx", axis=0, tiled=True)
+    gate_vals = jnp.dot(row_data, expert_in[0, 0], preferred_element_type=jnp.float32)
+    up_vals = jnp.dot(row_data, expert_in[0, 1], preferred_element_type=jnp.float32)
+    activated = ((up_vals + 1.0) * gate_vals * jax.nn.sigmoid(1.702 * gate_vals)).astype(
+        jnp.bfloat16
+    )
+    result = jnp.dot(activated, expert_out[0], preferred_element_type=jnp.float32)
+    result = jnp.where(mine != 0.0, result * mine, 0.0).astype(jnp.bfloat16)
+    halves = lax.psum_scatter(result, "tp", scatter_dimension=1, tiled=True)
+    total = lax.psum_scatter(halves, "ctx", scatter_dimension=0, tiled=True)
+    return (residual + total.astype(jnp.float32)).astype(jnp.bfloat16)
 
 
 def body(
@@ -81,6 +101,9 @@
         jnp.bfloat16
     )
     ctx_count = lax.axis_size("ctx")
+    weights = route_scores / jnp.sum(route_scores, -1, keepdims=True)
+    if ctx_count <= 16 and expert_in.shape[0] == 1:
+        return dense_experts(residual, normed, expert_in, expert_out, routes, weights)
     tp_count = lax.axis_size("tp")
     top_count = routes.shape[1]
     experts = ctx_count * expert_in.shape[0]
@@ -91,7 +114,6 @@
     before = jnp.cumsum(per_tok, axis=0) - per_tok
     slot_ids = jnp.sum(onehot * before[:, None, :], -1)
     flat_index = (routes * capacity + slot_ids).reshape(-1)
-    weights = route_scores / jnp.sum(route_scores, -1, keepdims=True)
     full_data = lax.all_gather(normed, "tp", axis=1, tiled=True)
     row_width = full_data.shape[1]
     spread = jnp.broadcast_to(full_data[:, None, :], (tok_rows, top_count, row_width)).reshape(

time: 389 us -> 326 us (0.84)
  blocking collectives: 120 us -> 33.4 us
  waiting for transfers between devices: 184 us -> 242 us
  local copies, waits for them, and re-layouts: 31.6 us -> 2.86 us
  starting transfers between devices: 7.82 us -> 2.53 us
    all_to_all x1 -> x0, blocking collectives: 109 us -> none  [body(): lax.all_to_all(outbox.reshape(ctx_count, 1, capacity, row_width), 'ctx',...]
    reduce_scatter x1 -> x2, waiting for transfers between devices: 42.3 us -> 146 us  [the longest x1 75.7 us: dense_experts(): halves = lax.psum_scatter(result, 'tp', scatter_dimension=1, tiled=True)]
    all_to_all x1 -> x0, waiting for transfers between devices: 86.7 us -> none  [body(): lax.all_to_all(result, 'ctx', split_axis=1, concat_axis=0, tiled=True)]
    all_gather x0 -> x1, waiting for transfers between devices: none -> 40.1 us  [dense_experts(): row_data = lax.all_gather(wide, 'ctx', axis=0, tiled=True)]
    all_gather x1 -> x2, blocking collectives: 6.35 us -> 28.5 us  [the longest x1 22 us: dense_experts(): every = lax.all_gather(spread, 'ctx', axis=0, tiled=True)]
    reshape x4 -> x0, local copies, waits for them, and re-layouts: 10.6 us -> none  [the longest x2 6.73 us: body(): returned.reshape(-1, d_model)[flat_index]]
    gather x1 -> x0, local copies, waits for them, and re-layouts: 7.36 us -> none  [body(): returned.reshape(-1, d_model)[flat_index]]
    scatter x1 -> x0, local copies, waits for them, and re-layouts: 6.77 us -> none  [body(): jnp.zeros((experts * capacity, row_width), jnp.bfloat16).at[flat_index]]
  transfers between devices with their start and end apart: 5 -> 6, of which waited for: 4 -> 5; matrix products, arithmetic and copies ran while one was open for 1% -> 1% of each run, Pallas kernels for 0% -> 0%
where the time goes in v1:
time: 326 us
  waiting for transfers between devices  242 us (74%)
  blocking collectives  33.4 us (10%)
  matrix products  27.4 us (8%)
  between operations  13.3 us (4%)
  other arithmetic  4.62 us (1%)
    reduce_scatter x1, waiting for transfers between devices, dense_experts(): halves = lax.psum_scatter(result, 'tp', scatter_dimension=1, tiled=True)  75.7 us
    reduce_scatter x1, waiting for transfers between devices, dense_experts(): total = lax.psum_scatter(halves, 'ctx', scatter_dimension=0, tiled=True)  69.9 us
    all_gather x1, waiting for transfers between devices, body(): lax.all_gather(out_proj, 'ctx', axis=1, tiled=True)  43.1 us
    all_gather x1, waiting for transfers between devices, dense_experts(): row_data = lax.all_gather(wide, 'ctx', axis=0, tiled=True)  40.1 us
    all_gather x1, blocking collectives, dense_experts(): every = lax.all_gather(spread, 'ctx', axis=0, tiled=True)  22 us
    reduce_scatter x1, waiting for transfers between devices, body(): lax.psum_scatter(head_partial.astype(jnp.bfloat16), 'tp', scatter_dimensi...  12 us
    dot_general x1, matrix products, dense_experts(): jnp.dot(row_data, expert_in[0, 0], preferred_element_type=jnp.float32)  7.99 us
    dot_general x1, matrix products, dense_experts(): jnp.dot(row_data, expert_in[0, 1], preferred_element_type=jnp.float32)  7.5 us
  transfers between devices with their start and end apart: 6, of which 5 were waited for; matrix products, arithmetic and copies ran while one was open for 1% of the time, Pallas kernels for 0%

profile of v1, /device:TPU:0, one launch (start us, length us, event | category | flops | bytes accessed | tf_op | source)
XLA Modules:
  0.0 325.7 jit_solution(13736150624122442300)
XLA Ops:
  6.5 0.0 copy-start
  6.5 0.0 all-gather.3.cloned.1.call-start
  6.5 0.7 all-gather.3.cloned.1.call-update
  7.3 0.0 reduce-scatter.4.cloned.1.call-start
  7.3 1.0 copy.23
  8.3 2.4 collective-permute-start
  10.7 0.1 and_and_fusion
  10.8 1.1 copy.25
  11.9 0.7 max.17
  12.7 0.0 collective-permute-done
  12.7 0.5 fusion.6
  13.2 0.1 broadcast_maximum_fusion
  13.3 0.4 fusion.9
  13.7 0.1 exponential_add_fusion
  13.8 0.6 convolution_convert_fusion.1
  14.4 0.0 copy-start.1
  14.4 0.0 copy-start.4
  14.4 0.0 copy-start.3
  14.5 0.0 copy-start.5
  14.5 43.1 %all-gather.3.cloned.1.call-done = bf16[1024,1536]{0,1:T(8,128)(2,1)} async-done(((bf16[1024,96]{0,1:T(8,128)(2,1)}), bf16[1024,1536]{0,1:T(8,128)(2,1)}) %all-gather.3.cloned.1.call-update) | async-done | bytes 3145744 | tf_op jit(solution)/shard_map/all_gather | solution.py:92
  57.6 3.8 %convolution_convert_fusion = bf16[128,1536]{1,0:T(8,128)(2,1)} fusion(bf16[128,1024]{0,1:T(8,128)(2,1)S(1)} %bitcast.47, bf16[1024,1536]{0,1:T(8,128)(2,1)} %all-gather.3.cloned.1.call-done), kind=kOutput, calls=%fused_computation.2 | convolution fusion | flops 402849792 | bytes 3801088 | tf_op jit(solution)/shard_map/dot_general | solution.py:90
  61.4 0.0 reduce-scatter.4.cloned.1.call-update
  61.4 0.0 all-gather.5.cloned.1.call-start
  61.5 12.0 %reduce-scatter.4.cloned.1.call-done = bf16[128,768]{1,0:T(8,128)(2,1)} async-done(((bf16[128,1536]{1,0:T(8,128)(2,1)}), bf16[128,768]{1,0:T(8,128)(2,1)}) %reduce-scatter.4.cloned.1.call-update) | async-done | bytes 196624 | tf_op jit(solution)/shard_map/reduce_scatter | solution.py:96
  73.5 0.0 copy-done.1
  73.5 1.1 multiply_reduce_fusion
  74.6 4.9 %psum.7 = f32[128]{0:T(128)S(1)} all-reduce(f32[128]{0:T(128)S(1)} %multiply_reduce_fusion), channel_id=1, replica_groups=mesh['ctx'=16,'tp'=2] {'tp'}, use_global_device_ids=true, to_apply=%region_6.7 | all-reduce | flops 128 | bytes 1024 | tf_op jit(solution)/shard_map/psum | solution.py:99
  79.5 0.0 copy-done.4
  79.5 1.0 multiply_convert_fusion.1
  80.6 6.5 %all_gather.14 = bf16[128,1536]{1,0:T(8,128)(2,1)} all-gather(bf16[128,768]{1,0:T(8,128)(2,1)S(1)} %multiply_convert_fusion.1), channel_id=1, replica_groups=mesh['ctx'=16,'tp'=2] {'tp'}, dimensions={1}, use_global_device_ids=true | all-gather | bytes 589824 | tf_op jit(solution)/shard_map/all_gather | solution.py:35
  87.0 0.0 all-gather.5.cloned.1.call-update
  87.0 0.0 reduce-scatter.6.cloned.1.call-start
  87.1 0.0 copy-done.3
  87.1 0.0 copy-done.5
  87.1 22.0 %all_gather.13 = f32[2048,16]{0,1:T(8,128)S(1)} all-gather(f32[128,16]{0,1:T(8,128)S(1)} %select_reduce_fusion), channel_id=1, replica_groups=mesh['ctx'=16,'tp'=2] {'ctx'}, dimensions={0}, use_global_device_ids=true | all-gather | bytes 139264 | tf_op jit(solution)/shard_map/all_gather | solution.py:33
  109.2 40.1 %all-gather.5.cloned.1.call-done = bf16[2048,1536]{1,0:T(8,128)(2,1)} async-done(((bf16[128,1536]{1,0:T(8,128)(2,1)}), bf16[2048,1536]{1,0:T(8,128)(2,1)}) %all-gather.5.cloned.1.call-update) | async-done | bytes 6291472 | tf_op jit(solution)/shard_map/all_gather | solution.py:36
  149.3 8.0 %fusion.1 = f32[2048,768]{1,0:T(8,128)S(1)} fusion(bf16[2048,1536]{1,0:T(8,128)(2,1)} %all-gather.5.cloned.1.call-done, bf16[1,2,1536,768]{3,2,1,0:T(8,128)(2,1)} %param.16), kind=kOutput, calls=%fused_computation.4 | convolution fusion | flops 4831838208 | bytes 14942208 | tf_op jit(solution)/shard_map/dot_general | solution.py:37
  157.3 0.0 copy-done.6
  157.3 7.5 %multiply_convert_fusion = bf16[2048,768]{1,0:T(8,128)(2,1)S(1)} fusion(f32[2048,768]{1,0:T(8,128)S(1)} %fusion.1, bf16[2048,1536]{1,0:T(8,128)(2,1)S(1)} %copy-done.6, bf16[1,2,1536,768]{3,2,1,0:T(8,128)(2,1)} %param.16), kind=kOutput, calls=%fused_computation.1 | convolution fusion | flops 4844421120 | bytes 18087936 | tf_op jit(solution)/shard_map/dot_general | solution.py:38
  164.8 0.0 copy-done
  164.8 7.0 %select_convert_fusion = bf16[2048,1536]{1,0:T(8,128)(2,1)} fusion(bf16[2048,768]{1,0:T(8,128)(2,1)S(1)} %multiply_convert_fusion, f32[2048]{0:T(1024)S(1)} %bitcast.48, pred[2048]{0:T(1024)(128)(4,1)S(1)} %get-tuple-element.5, bf16[1,768,1536]{2,1,0:T(8,128)(2,1)S(1)} %copy-done), kind=kOutput, calls=%fused_computation | convolution fusion | flops 4841275392 | bytes 11806720 | tf_op jit(solution)/shard_map/dot_general | solution.py:42
  171.8 0.0 reduce-scatter.6.cloned.1.call-update
  171.8 0.0 copy-start.2
  171.8 0.0 reduce-scatter.8.cloned.1.call-start
  171.9 75.7 %reduce-scatter.6.cloned.1.call-done = bf16[2048,768]{1,0:T(8,128)(2,1)} async-done(((bf16[2048,1536]{1,0:T(8,128)(2,1)}), bf16[2048,768]{1,0:T(8,128)(2,1)}) %reduce-scatter.6.cloned.1.call-update) | async-done | bytes 3145744 | tf_op jit(solution)/shard_map/reduce_scatter | solution.py:44
  247.6 0.0 reduce-scatter.8.cloned.1.call-update
  247.6 69.9 %reduce-scatter.8.cloned.1.call-done = bf16[128,768]{1,0:T(8,128)(2,1)} async-done(((bf16[2048,768]{1,0:T(8,128)(2,1)}), bf16[128,768]{1,0:T(8,128)(2,1)}) %reduce-scatter.8.cloned.1.call-update) | async-done | bytes 196624 | tf_op jit(solution)/shard_map/reduce_scatter | solution.py:45
  317.5 1.7 add_convert_fusion
  (10 shorter events, 0.1 us)
Async XLA Ops:
  6.5 158.3 %copy-start = (bf16[1,768,1536]{2,1,0:T(8,128)(2,1)S(1)}, bf16[1,768,1536]{2,1,0:T(8,128)(2,1)}, u32[]{:S(2)}) copy-start(bf16[1,768,1536]{2,1,0:T(8,128)(2,1)} %param.17) | copy-start | bytes 7077892
  6.5 51.0 %all-gather.3.cloned.1.call-start = ((), (), s32[]{:S(2)}) async-start(), calls=%async_computation.3 | async-start | bytes 3342336 | tf_op jit(solution)/shard_map/all_gather | solution.py:92
  7.3 66.2 %reduce-scatter.4.cloned.1.call-start = ((), (), s32[]{:S(2)}) async-start(), calls=%async_computation.4 | async-start | bytes 589824 | tf_op jit(solution)/shard_map/reduce_scatter | solution.py:96
  8.3 4.4 %collective-permute-start = (bf16[128,2,128]{0,2,1:T(8,128)(2,1)S(1)}, bf16[128,2,128]{0,2,1:T(8,128)(2,1)S(1)}, u32[]{:S(2)}, u32[]{:S(2)}) collective-permute-start(bf16[128,2,128]{0,2,1:T(8,128)(2,1)S(1)} %copy.23), channel_id=1, source_target_pairs={{0,2},{2,4},{4,6},{6,8},{8,10},{10,12},{12,14},{14,16},{16,18},{18... | collective-permute-start | bytes 196616 | tf_op jit(solution)/shard_map/ppermute | solution.py:12
  14.4 59.1 %copy-start.1 = (bf16[128,768]{1,0:T(8,128)(2,1)S(1)}, bf16[128,768]{1,0:T(8,128)(2,1)}, u32[]{:S(2)}) copy-start(bf16[128,768]{1,0:T(8,128)(2,1)} %param.10) | copy-start | bytes 589828
  14.4 65.1 %copy-start.4 = (f32[768]{0:T(1024)S(1)}, f32[768]{0:T(1024)}, u32[]{:S(2)}) copy-start(f32[768]{0:T(1024)} %param.15) | copy-start | bytes 9220
  14.4 72.6 %copy-start.3 = (f32[128,4]{0,1:T(4,128)S(1)}, f32[128,4]{0,1:T(4,128)}, u32[]{:S(2)}) copy-start(f32[128,4]{0,1:T(4,128)} %param.19) | copy-start | bytes 6148
  14.5 72.7 %copy-start.5 = (s32[128,4]{0,1:T(4,128)S(1)}, s32[128,4]{0,1:T(4,128)}, u32[]{:S(2)}) copy-start(s32[128,4]{0,1:T(4,128)} %param.18) | copy-start | bytes 6148
  61.4 87.9 %all-gather.5.cloned.1.call-start = ((), (), s32[]{:S(2)}) async-start(), calls=%async_computation.5 | async-start | bytes 6684672 | tf_op jit(solution)/shard_map/all_gather | solution.py:36
  87.0 160.6 %reduce-scatter.6.cloned.1.call-start = ((), (), s32[]{:S(2)}) async-start(), calls=%async_computation.6 | async-start | bytes 9437184 | tf_op jit(solution)/shard_map/reduce_scatter | solution.py:44
  149.3 8.0 %copy-start.6 = (bf16[2048,1536]{1,0:T(8,128)(2,1)S(1)}, bf16[2048,1536]{1,0:T(8,128)(2,1)}, u32[]{:S(2)}) copy-start(bf16[2048,1536]{1,0:T(8,128)(2,1)} %all-gather.5.cloned.1.call-done) | copy-start | bytes 18874372
  171.8 145.7 %copy-start.2 = (bf16[128,768]{1,0:T(8,128)(2,1)S(1)}, bf16[128,768]{1,0:T(8,128)(2,1)}, u32[]{:S(2)}) copy-start(bf16[128,768]{1,0:T(8,128)(2,1)} %reduce-scatter.4.cloned.1.call-done) | copy-start | bytes 589828
  171.8 145.7 %reduce-scatter.8.cloned.1.call-start = ((), (), s32[]{:S(2)}) async-start(), calls=%async_computation.7 | async-start | bytes 3342336 | tf_op jit(solution)/shard_map/reduce_scatter | solution.py:45
Sparse Core Ops, SparseCore 0:
  9.6 47.8 all-gather.2
  61.5 11.9 reduce-scatter.3
  87.2 62.0 all-gather.4
  171.9 75.6 reduce-scatter.5
  251.3 66.2 reduce-scatter.7

commit v2 on v0

--- a/solution.py
+++ b/solution.py
@@ -1,6 +1,8 @@
 import jax
 import jax.numpy as jnp
 from jax import lax
+from jax.experimental import pallas as pl
+from jax.experimental.pallas import tpu as pltpu
 from jax.sharding import PartitionSpec as P
 
 WINDOW_KEYS = 128
@@ -24,6 +26,282 @@
     probs = (expvals / denominator[..., None]).astype(jnp.bfloat16)
     mixed = jnp.einsum("gqrs,sgd->rgqd", probs, value_blk, preferred_element_type=jnp.float32)
     return mixed.astype(jnp.bfloat16)
+
+
+def expert_kernel(
+    normed_ref, mine_ref, residual_ref, w_in_hbm, w_out_hbm, out_ref,
+    full, part, w_in, w_out, act, from_core, from_two, from_one, from_z,
+    load_sem, own_sem,
+    gz_send, gz_recv, g1_send, g1_recv, g2_send, g2_recv, g3_send, g3_recv,
+    rc_send, rc_recv, r2_send, r2_recv, r1_send, r1_recv, rz_send, rz_recv,
+):
+    ctx, x = lax.axis_index("ctx"), lax.axis_index("tp")
+    z, y, c = ctx // 4, (ctx // 2) % 2, ctx % 2
+    rows = normed_ref.shape[0]
+    half = rows // 2
+    width = normed_ref.shape[1]
+    there = [z, z + 1 - 2 * (z % 2), z + 2 - 4 * (z // 2), 3 - z]
+
+    def place(z_at, y_at, c_at):
+        return z_at * 4 + y_at * 2 + c_at
+
+    core_dev, y_dev, x_dev = (place(z, y, 1 - c), x), (place(z, 1 - y, c), x), (ctx, 1 - x)
+    z_devs = [None] + [(place(there[o], y, c), x) for o in range(1, 4)]
+    first_dev, second_dev = (y_dev, x_dev), (x_dev, y_dev)
+
+    def span(z_at, y_at, c_at, chunk):
+        return pl.ds(pl.multiple_of(place(z_at, y_at, c_at) * rows + chunk * half, half), half)
+
+    def block(z_at, y_at, c_at):
+        return pl.ds(pl.multiple_of(place(z_at, y_at, c_at) * rows, rows), rows)
+
+    def remote(src, dst, send, recv, device):
+        return pltpu.make_async_remote_copy(
+            src_ref=src, dst_ref=dst, send_sem=send, recv_sem=recv,
+            device_id=device, device_id_type=pl.DeviceIdType.MESH,
+        )
+
+    loads = [
+        pltpu.make_async_copy(w_in_hbm, w_in, load_sem.at[0]),
+        pltpu.make_async_copy(w_out_hbm, w_out, load_sem.at[1]),
+    ]
+    for load in loads:
+        load.start()
+    barrier = pltpu.get_barrier_semaphore()
+    peers = [core_dev, y_dev, x_dev] + z_devs[1:]
+    for peer in peers:
+        pl.semaphore_signal(barrier, inc=1, device_id=peer, device_id_type=pl.DeviceIdType.MESH)
+    pl.semaphore_wait(barrier, len(peers))
+
+    def piece(chunk, o, one, two, core):
+        y_at = y if (one if chunk == 0 else two) == 0 else 1 - y
+        x_at = x if (two if chunk == 0 else one) == 0 else 1 - x
+        c_at = c if core == 0 else 1 - c
+        return full.at[x_at, span(there[o], y_at, c_at, chunk)]
+
+    sends = []
+
+    def send(src, dst, s_sem, r_sem, device):
+        copy = remote(src, dst, s_sem, r_sem, device)
+        copy.start()
+        sends.append(copy)
+
+    own = normed_ref
+    own_copies = []
+    for chunk in range(2):
+        src = own.at[pl.ds(chunk * half, half)]
+        dst = piece(chunk, 0, 0, 0, 0)
+        for o in (3, 2, 1):
+            send(src, dst, gz_send.at[chunk, o], gz_recv.at[chunk, o], z_devs[o])
+        keep = pltpu.make_async_copy(src, dst, own_sem.at[chunk])
+        keep.start()
+        own_copies.append(keep)
+
+    def pass_on(chunk, o, one, two):
+        src = own.at[pl.ds(chunk * half, half)] if (o, one, two) == (0, 0, 0) else piece(chunk, o, one, two, 0)
+        dst = piece(chunk, o, one, two, 0)
+        if one == 0 and two == 0:
+            send(src, dst, g1_send.at[chunk, o], g1_recv.at[chunk, o], first_dev[chunk])
+        if two == 0:
+            send(src, dst, g2_send.at[chunk, o, one], g2_recv.at[chunk, o, one], second_dev[chunk])
+        send(src, dst, g3_send.at[chunk, o, one, two], g3_recv.at[chunk, o, one, two], core_dev)
+
+    def arrive(dst, s_sem, r_sem):
+        remote(dst, dst, s_sem, r_sem, core_dev).wait_recv()
+
+    def gather(o):
+        for chunk in range(2):
+            if o:
+                arrive(piece(chunk, o, 0, 0, 0), gz_send.at[chunk, o], gz_recv.at[chunk, o])
+            pass_on(chunk, o, 0, 0)
+        for chunk in range(2):
+            arrive(piece(chunk, o, 1, 0, 0), g1_send.at[chunk, o], g1_recv.at[chunk, o])
+            pass_on(chunk, o, 1, 0)
+        for one in range(2):
+            for chunk in range(2):
+                arrive(piece(chunk, o, one, 1, 0), g2_send.at[chunk, o, one], g2_recv.at[chunk, o, one])
+                pass_on(chunk, o, one, 1)
+
+    def gather_core(o):
+        for chunk in range(2):
+            for one in range(2):
+                for two in range(2):
+                    arrive(
+                        piece(chunk, o, one, two, 1),
+                        g3_send.at[chunk, o, one, two],
+                        g3_recv.at[chunk, o, one, two],
+                    )
+
+    group = 4 * rows
+
+    def compute(o):
+        base = pl.multiple_of(there[o] * group, group)
+        near = pl.ds(base, group)
+        tile = 256
+
+        @pl.loop(0, width // tile)
+        def _(step):
+            cols = pl.ds(pl.multiple_of(step * tile, tile), tile)
+
+            def project(which):
+                return jnp.dot(
+                    full[0, near], w_in[which, pl.ds(0, width), cols], preferred_element_type=jnp.float32
+                ) + jnp.dot(
+                    full[1, near], w_in[which, pl.ds(width, width), cols], preferred_element_type=jnp.float32
+                )
+
+            gate, up = project(0), project(1)
+            act[:, cols] = ((up + 1.0) * gate * jax.nn.sigmoid(1.702 * gate)).astype(jnp.bfloat16)
+
+        for at in range(2):
+
+            @pl.loop(0, width // tile)
+            def _(step):
+                start = pl.multiple_of(step * tile, tile)
+                cols = pl.ds(start, tile)
+                wide = pl.ds(pl.multiple_of(at * width + step * tile, tile), tile)
+                value = jnp.dot(act[...], w_out[:, wide], preferred_element_type=jnp.float32)
+                part[at, near, cols] = (value * mine_ref[near]).astype(jnp.bfloat16)
+
+        for x_at in range(2):
+            for y_at in range(2):
+                send(
+                    part.at[x_at, block(there[o], y_at, 1 - c)], from_core.at[o, x_at, y_at],
+                    rc_send.at[o, x_at, y_at], rc_recv.at[o, x_at, y_at], core_dev,
+                )
+
+    def add(x_at, where, ref):
+        part[x_at, where] = (
+            part[x_at, where].astype(jnp.float32) + ref[...].astype(jnp.float32)
+        ).astype(jnp.bfloat16)
+
+    def reduce_core(o):
+        for x_at in range(2):
+            for y_at in range(2):
+                got = from_core.at[o, x_at, y_at]
+                arrive(got, rc_send.at[o, x_at, y_at], rc_recv.at[o, x_at, y_at])
+                add(x_at, block(there[o], y_at, c), got)
+        for k in range(2):
+            send(
+                part.at[1 - x, span(there[o], k, c, 0)], from_two.at[0, o, k],
+                r2_send.at[0, o, k], r2_recv.at[0, o, k], x_dev,
+            )
+            send(
+                part.at[k, span(there[o], 1 - y, c, 1)], from_two.at[1, o, k],
+                r2_send.at[1, o, k], r2_recv.at[1, o, k], y_dev,
+            )
+
+    def reduce_two(o):
+        for k in range(2):
+            for chunk in range(2):
+                got = from_two.at[chunk, o, k]
+                arrive(got, r2_send.at[chunk, o, k], r2_recv.at[chunk, o, k])
+                if chunk == 0:
+                    add(x, span(there[o], k, c, 0), got)
+                else:
+                    add(k, span(there[o], y, c, 1), got)
+        send(
+            part.at[x, span(there[o], 1 - y, c, 0)], from_one.at[0, o],
+            r1_send.at[0, o], r1_recv.at[0, o], y_dev,
+        )
+        send(
+            part.at[1 - x, span(there[o], y, c, 1)], from_one.at[1, o],
+            r1_send.at[1, o], r1_recv.at[1, o], x_dev,
+        )
+
+    def reduce_one(o):
+        for chunk in range(2):
+            got = from_one.at[chunk, o]
+            arrive(got, r1_send.at[chunk, o], r1_recv.at[chunk, o])
+            add(x, span(there[o], y, c, chunk), got)
+            if o:
+                send(
+                    part.at[x, span(there[o], y, c, chunk)], from_z.at[o, chunk],
+                    rz_send.at[o, chunk], rz_recv.at[o, chunk], z_devs[o],
+                )
+
+    gather(0)
+    for keep in own_copies:
+        keep.wait()
+    for load in loads:
+        load.wait()
+    gather_core(0)
+    compute(0)
+    gather(1)
+    gather_core(1)
+    compute(1)
+    reduce_core(0)
+    gather(2)
+    gather_core(2)
+    compute(2)
+    reduce_core(1)
+    reduce_two(0)
+    gather(3)
+    gather_core(3)
+    compute(3)
+    reduce_core(2)
+    reduce_two(1)
+    reduce_one(0)
+    reduce_core(3)
+    reduce_two(2)
+    reduce_one(1)
+    reduce_two(3)
+    reduce_one(2)
+    reduce_one(3)
+    for chunk in range(2):
+        mine_rows = pl.ds(chunk * half, half)
+        total = residual_ref[mine_rows] + part[x, span(z, y, c, chunk)].astype(jnp.float32)
+        for o in range(1, 4):
+            arrive(from_z.at[o, chunk], rz_send.at[o, chunk], rz_recv.at[o, chunk])
+            total = total + from_z[o, chunk].astype(jnp.float32)
+        out_ref[mine_rows] = total.astype(jnp.bfloat16)
+    for copy in sends:
+        copy.wait_send()
+
+
+def dense_experts(residual, normed, expert_in, expert_out, routes, weights):
+    experts = lax.axis_size("ctx")
+    rows, width = normed.shape
+    chosen = routes[:, :, None] == jnp.arange(experts, dtype=jnp.int32)
+    spread = jnp.sum(jnp.where(chosen, weights[:, :, None], 0.0), 1)
+    every = lax.all_gather(spread, "ctx", axis=0, tiled=True)
+    mine = lax.dynamic_slice_in_dim(every, lax.axis_index("ctx"), 1, 1)
+    dma = pltpu.SemaphoreType.DMA
+    bf16 = jnp.bfloat16
+    vmem = pl.BlockSpec(memory_space=pltpu.VMEM)
+    total = experts * rows
+    hidden = expert_in.shape[3]
+    flops = 2 * total * hidden * width * 2 * 3
+    return pl.pallas_call(
+        expert_kernel,
+        out_shape=jax.ShapeDtypeStruct((rows, width), bf16),
+        in_specs=[vmem] * 3 + [pl.BlockSpec(memory_space=pl.ANY)] * 2,
+        out_specs=vmem,
+        scratch_shapes=[
+            pltpu.VMEM((2, total, width), bf16),
+            pltpu.VMEM((2, total, width), bf16),
+            pltpu.VMEM((2, 2 * width, hidden), bf16),
+            pltpu.VMEM((hidden, 2 * width), bf16),
+            pltpu.VMEM((4 * rows, hidden), bf16),
+            pltpu.VMEM((4, 2, 2, rows, width), bf16),
+            pltpu.VMEM((2, 4, 2, rows // 2, width), bf16),
+            pltpu.VMEM((2, 4, rows // 2, width), bf16),
+            pltpu.VMEM((4, 2, rows // 2, width), bf16),
+            dma((2,)),
+            dma((2,)),
+        ]
+        + [dma((2, 4))] * 4
+        + [dma((2, 4, 2))] * 2
+        + [dma((2, 4, 2, 2))] * 2
+        + [dma((4, 2, 2))] * 2
+        + [dma((2, 4, 2))] * 2
+        + [dma((2, 4))] * 2
+        + [dma((4, 2))] * 2,
+        compiler_params=pltpu.CompilerParams(
+            collective_id=1, has_side_effects=True, vmem_limit_bytes=50 * 2**20
+        ),
+        cost_estimate=pl.CostEstimate(flops=flops, bytes_accessed=8 * 2**20, transcendentals=0),
+    )(normed, mine, residual, expert_in[0], expert_out[0])
 
 
 def body(
@@ -81,6 +359,9 @@
         jnp.bfloat16
     )
     ctx_count = lax.axis_size("ctx")
+    weights = route_scores / jnp.sum(route_scores, -1, keepdims=True)
+    if ctx_count == 16 and lax.axis_size("tp") == 2 and expert_in.shape[0] == 1:
+        return dense_experts(residual, normed, expert_in, expert_out, routes, weights)
     tp_count = lax.axis_size("tp")
     top_count = routes.shape[1]
     experts = ctx_count * expert_in.shape[0]
@@ -88,10 +369,13 @@
     quarter_w = d_model // tp_count
     onehot = (routes[:, :, None] == jnp.arange(experts, dtype=jnp.int32)).astype(jnp.int32)
     per_tok = jnp.sum(onehot, 1)
-    before = jnp.cumsum(per_tok, axis=0) - per_tok
+    position = jnp.arange(tok_rows, dtype=jnp.int32)
+    earlier_rows = (position[:, None] > position[None, :]).astype(jnp.bfloat16)
+    before = jnp.dot(
+        earlier_rows, per_tok.astype(jnp.bfloat16), preferred_element_type=jnp.float32
+    ).astype(jnp.int32)
     slot_ids = jnp.sum(onehot * before[:, None, :], -1)
     flat_index = (routes * capacity + slot_ids).reshape(-1)
-    weights = route_scores / jnp.sum(route_scores, -1, keepdims=True)
     full_data = lax.all_gather(normed, "tp", axis=1, tiled=True)
     row_width = full_data.shape[1]
     spread = jnp.broadcast_to(full_data[:, None, :], (tok_rows, top_count, row_width)).reshape(

time: 389 us -> 209 us (0.54)
  waiting for transfers between devices: 184 us -> 43.9 us
  Pallas kernels: 0 us -> 109 us
  blocking collectives: 120 us -> 27.1 us
  local copies, waits for them, and re-layouts: 31.6 us -> 3.95 us
  matrix products: 26 us -> 4.95 us
  starting transfers between devices: 7.82 us -> 2.4 us
    all_to_all x1 -> x0, blocking collectives: 109 us -> none  [body(): lax.all_to_all(outbox.reshape(ctx_count, 1, capacity, row_width), 'ctx',...]
    pallas_call x0 -> x1, Pallas kernels: none -> 109 us  [dense_experts(): pl.pallas_call(expert_kernel, out_shape=jax.ShapeDtypeStruct((rows, width...]
    all_to_all x1 -> x0, waiting for transfers between devices: 86.7 us -> none  [body(): lax.all_to_all(result, 'ctx', split_axis=1, concat_axis=0, tiled=True)]
    reduce_scatter x1 -> x0, waiting for transfers between devices: 42.3 us -> none  [body(): lax.psum_scatter(picked.astype(jnp.float32).astype(jnp.bfloat16), 'tp', s...]
    dot_general x2 -> x0, matrix products: 21 us -> none  [the longest x1 13.9 us: body(): jnp.dot(activated, expert_out[0], preferred_element_type=jnp.float32)]
    all_gather x1, blocking collectives: 6.35 us -> 22.2 us  [dense_experts(): every = lax.all_gather(spread, 'ctx', axis=0, tiled=True)]
    reduce_scatter x1, waiting for transfers between devices: 11.4 us -> 0.02 us  [body(): lax.psum_scatter(head_partial.astype(jnp.bfloat16), 'tp', scatter_dimensi...]
    reshape x4 -> x0, local copies, waits for them, and re-layouts: 10.6 us -> none  [the longest x2 6.73 us: body(): returned.reshape(-1, d_model)[flat_index]]
  transfers between devices with their start and end apart: 5 -> 3, of which waited for: 4 -> 1; matrix products, arithmetic and copies ran while one was open for 1% -> 2% of each run, Pallas kernels for 0% -> 0%
where the time goes in v2:
time: 209 us; the launch traced here: 207 us
  Pallas kernels  109 us (52%)
  waiting for transfers between devices  43.9 us (21%)
  blocking collectives  27.1 us (13%)
  between operations  13.5 us (6%)
  matrix products  4.95 us (2%)
  local copies, waits for them, and re-layouts  3.95 us (2%)
  other arithmetic  2.9 us (1%)
  starting transfers between devices  2.4 us (1%)
    pallas_call x1, Pallas kernels, dense_experts(): pl.pallas_call(expert_kernel, out_shape=jax.ShapeDtypeStruct((rows, width...  109 us
    all_gather x1, waiting for transfers between devices, body(): lax.all_gather(out_proj, 'ctx', axis=1, tiled=True)  43.1 us
    all_gather x1, blocking collectives, dense_experts(): every = lax.all_gather(spread, 'ctx', axis=0, tiled=True)  22.2 us
    psum x1, blocking collectives, body(): square_total = lax.psum(jnp.sum(residual * residual, -1), 'tp')  4.93 us
  transfers between devices with their start and end apart: 3, of which 1 were waited for; matrix products, arithmetic and copies ran while one was open for 2% of the time, Pallas kernels for 0%

profile of v2, /device:TPU:0, one launch (start us, length us, event | category | flops | bytes accessed | tf_op | source)
XLA Modules:
  0.0 207.4 jit_solution(9099300730626053803)
XLA Ops:
  6.5 0.0 all-gather.2.cloned.1.call-start
  6.5 0.7 all-gather.2.cloned.1.call-update
  7.3 0.0 reduce-scatter.2.cloned.1.call-start
  7.3 1.0 copy.23
  8.3 2.4 %collective-permute-start = (bf16[128,2,128]{0,2,1:T(8,128)(2,1)S(1)}, bf16[128,2,128]{0,2,1:T(8,128)(2,1)S(1)}, u32[]{:S(2)}, u32[]{:S(2)}) collective-permute-start(bf16[128,2,128]{0,2,1:T(8,128)(2,1)S(1)} %copy.23), channel_id=1, source_target_pairs={{0,2},{2,4},{4,6},{6,8},{8,10},{10,12},{12,14},{14,16},{16,18},{18... | collective-permute-start | bytes 196616 | tf_op jit(solution)/shard_map/ppermute | solution.py:14
  10.7 0.1 and_and_fusion
  10.8 1.1 copy.25
  11.9 0.7 max.17
  12.7 0.0 collective-permute-done
  12.7 0.5 fusion
  13.2 0.1 broadcast_maximum_fusion
  13.2 0.4 fusion.3
  13.7 0.1 exponential_add_fusion
  13.8 0.6 convolution_convert_fusion.1
  14.4 43.1 %all-gather.2.cloned.1.call-done = bf16[1024,1536]{0,1:T(8,128)(2,1)} async-done(((bf16[1024,96]{0,1:T(8,128)(2,1)}), bf16[1024,1536]{0,1:T(8,128)(2,1)}) %all-gather.2.cloned.1.call-update) | async-done | bytes 3145744 | tf_op jit(solution)/shard_map/all_gather | solution.py:350
  57.6 0.0 copy-start.1
  57.6 0.0 copy-start.3
  57.6 3.8 %convolution_convert_fusion = bf16[128,1536]{1,0:T(8,128)(2,1)} fusion(bf16[128,1024]{0,1:T(8,128)(2,1)S(1)} %bitcast.36, bf16[1024,1536]{0,1:T(8,128)(2,1)} %all-gather.2.cloned.1.call-done), kind=kOutput, calls=%fused_computation | convolution fusion | flops 402849792 | bytes 3801088 | tf_op jit(solution)/shard_map/dot_general | solution.py:348
  61.4 0.0 copy-start
  61.4 0.0 reduce-scatter.2.cloned.1.call-update
  61.4 0.0 copy-start.2
  61.4 0.0 copy-done.1
  61.5 0.0 copy-done.3
  61.5 0.1 copy.27
  61.6 22.2 %all_gather.7 = f32[2048,16]{1,0:T(8,128)S(1)} all-gather(f32[128,16]{1,0:T(8,128)S(1)} %copy.27), channel_id=1, replica_groups=mesh['ctx'=16,'tp'=2] {'ctx'}, dimensions={0}, use_global_device_ids=true | all-gather | bytes 139264 | tf_op jit(solution)/shard_map/all_gather | solution.py:267
  83.8 0.3 constant_dynamic-slice_fusion.mine_ref
  84.1 0.0 reduce-scatter.2.cloned.1.call-done
  84.2 0.0 copy-done
  84.2 1.1 convert_add_fusion
  85.2 4.9 %psum.7 = f32[128]{0:T(128)S(1)} all-reduce(f32[128]{0:T(128)S(1)} %get-tuple-element.6), channel_id=1, replica_groups=mesh['ctx'=16,'tp'=2] {'tp'}, use_global_device_ids=true, to_apply=%region_4.5 | all-reduce | flops 128 | bytes 1024 | tf_op jit(solution)/shard_map/psum | solution.py:357
  90.2 0.0 copy-done.2
  90.2 1.0 multiply_convert_fusion.normed_ref
  91.2 108.7 %shard_map.100 = bf16[128,768]{1,0:T(8,128)(2,1)S(1)} custom-call(bf16[128,768]{1,0:T(8,128)(2,1)S(1)} %multiply_convert_fusion.normed_ref, f32[2048,1]{1,0:T(8,128)S(1)} %constant_dynamic-slice_fusion.mine_ref, f32[128,768]{1,0:T(8,128)S(1)} %get-tuple-element.5.residual_ref, bf16[2,1536,768]{2,1,0:T(8,128)(2,1)} %bitcast.37, bf16[768,1536]{1,0:T(8,128)(2,1)} %bitcast.38), custom_call_target="tpu_custom_call" | custom-call | flops 14495514624 | bytes 8388608 | tf_op jit(solution)/shard_map/pallas_call | solution.py:275
  199.9 0.7 copy.32
  (7 shorter events, 0.1 us)
Async XLA Ops:
  6.5 51.0 %all-gather.2.cloned.1.call-start = ((), (), s32[]{:S(2)}) async-start(), calls=%async_computation.1 | async-start | bytes 3342336 | tf_op jit(solution)/shard_map/all_gather | solution.py:350
  7.3 76.9 %reduce-scatter.2.cloned.1.call-start = ((), (), s32[]{:S(2)}) async-start(), calls=%async_computation.2 | async-start | bytes 589824 | tf_op jit(solution)/shard_map/reduce_scatter | solution.py:354
  8.3 4.4 %collective-permute-start = (bf16[128,2,128]{0,2,1:T(8,128)(2,1)S(1)}, bf16[128,2,128]{0,2,1:T(8,128)(2,1)S(1)}, u32[]{:S(2)}, u32[]{:S(2)}) collective-permute-start(bf16[128,2,128]{0,2,1:T(8,128)(2,1)S(1)} %copy.23), channel_id=1, source_target_pairs={{0,2},{2,4},{4,6},{6,8},{8,10},{10,12},{12,14},{14,16},{16,18},{18... | collective-permute-start | bytes 196616 | tf_op jit(solution)/shard_map/ppermute | solution.py:14
  57.6 3.9 %copy-start.1 = (f32[128,4]{0,1:T(4,128)S(1)}, f32[128,4]{0,1:T(4,128)}, u32[]{:S(2)}) copy-start(f32[128,4]{0,1:T(4,128)} %param.19) | copy-start | bytes 6148
  57.6 3.9 %copy-start.3 = (s32[128,4]{0,1:T(4,128)S(1)}, s32[128,4]{0,1:T(4,128)}, u32[]{:S(2)}) copy-start(s32[128,4]{0,1:T(4,128)} %param.18) | copy-start | bytes 6148
  61.4 22.8 %copy-start = (bf16[128,768]{1,0:T(8,128)(2,1)S(1)}, bf16[128,768]{1,0:T(8,128)(2,1)}, u32[]{:S(2)}) copy-start(bf16[128,768]{1,0:T(8,128)(2,1)} %param.10) | copy-start | bytes 589828
  61.4 28.8 %copy-start.2 = (f32[768]{0:T(1024)S(1)}, f32[768]{0:T(1024)}, u32[]{:S(2)}) copy-start(f32[768]{0:T(1024)} %param.15) | copy-start | bytes 9220
Sparse Core Ops, SparseCore 0:
  9.6 47.8 all-gather.1
  61.5 11.9 reduce-scatter.1

commit v3 on v2

--- a/solution.py
+++ b/solution.py
@@ -259,13 +259,243 @@
         copy.wait_send()
 
 
-def dense_experts(residual, normed, expert_in, expert_out, routes, weights):
+def front_kernel(
+    q_ref, kv_ref, sink_ref, proj_ref, spread_ref, hidden_ref, gain_ref,
+    residual_ref, normed_ref, table_ref,
+    keys, proj, att, sums, outgoing, incoming, square_out, square_in,
+    own_sem, kv_send, kv_recv, x_send, x_recv, s_send, s_recv,
+    pz_send, pz_recv, py_send, py_recv, pc_send, pc_recv,
+    wz_send, wz_recv, wy_send, wy_recv, wc_send, wc_recv,
+):
+    ctx, x = lax.axis_index("ctx"), lax.axis_index("tp")
+    z, y, c = ctx // 4, (ctx // 2) % 2, ctx % 2
+    there = [z, z + 1 - 2 * (z % 2), z + 2 - 4 * (z // 2), 3 - z]
+    rows = q_ref.shape[0]
+    wide = proj_ref.shape[0]
+    count = 16
+
+    def place(z_at, y_at, c_at):
+        return z_at * 4 + y_at * 2 + c_at
+
+    core_dev, y_dev, x_dev = (place(z, y, 1 - c), x), (place(z, 1 - y, c), x), (ctx, 1 - x)
+    z_devs = [None] + [(place(there[o], y, c), x) for o in range(1, 4)]
+    next_dev, last_dev = ((ctx + 1) % count, x), ((ctx + count - 1) % count, x)
+
+    def remote(src, dst, send, recv, device):
+        return pltpu.make_async_remote_copy(
+            src_ref=src, dst_ref=dst, send_sem=send, recv_sem=recv,
+            device_id=device, device_id_type=pl.DeviceIdType.MESH,
+        )
+
+    def columns(z_at, y_at, c_at):
+        return proj.at[pl.ds(pl.multiple_of(place(z_at, y_at, c_at) * wide, 16), wide)]
+
+    def share(z_at, y_at, c_at):
+        return table_ref.at[place(z_at, y_at, c_at)]
+
+    barrier = pltpu.get_barrier_semaphore()
+    peers = [core_dev, y_dev, x_dev, next_dev, last_dev] + z_devs[1:]
+    for peer in peers:
+        pl.semaphore_signal(barrier, inc=1, device_id=peer, device_id_type=pl.DeviceIdType.MESH)
+    pl.semaphore_wait(barrier, len(peers))
+
+    sends = []
+
+    def send(src, dst, s_sem, r_sem, device):
+        copy = remote(src, dst, s_sem, r_sem, device)
+        copy.start()
+        sends.append(copy)
+
+    def arrive(dst, s_sem, r_sem):
+        remote(dst, dst, s_sem, r_sem, core_dev).wait_recv()
+
+    send(kv_ref, keys.at[pl.ds(0, rows)], kv_send.at[0], kv_recv.at[0], next_dev)
+    for o in (3, 2, 1):
+        send(proj_ref, columns(z, y, c), pz_send.at[o], pz_recv.at[o], z_devs[o])
+        send(spread_ref, share(z, y, c), wz_send.at[o], wz_recv.at[o], z_devs[o])
+    keeps = [
+        pltpu.make_async_copy(kv_ref, keys.at[pl.ds(rows, rows)], own_sem.at[0]),
+        pltpu.make_async_copy(proj_ref, columns(z, y, c), own_sem.at[1]),
+        pltpu.make_async_copy(spread_ref, share(z, y, c), own_sem.at[2]),
+    ]
+    for keep in keeps:
+        keep.start()
+
+    def pass_on(o, y_flip):
+        y_at = 1 - y if y_flip else y
+        own = o == 0 and not y_flip
+        src = proj_ref if own else columns(there[o], y_at, c)
+        small = spread_ref if own else share(there[o], y_at, c)
+        if not y_flip:
+            send(src, columns(there[o], y_at, c), py_send.at[o], py_recv.at[o], y_dev)
+            send(small, share(there[o], y_at, c), wy_send.at[o], wy_recv.at[o], y_dev)
+        send(src, columns(there[o], y_at, c), pc_send.at[o, y_flip], pc_recv.at[o, y_flip], core_dev)
+        send(small, share(there[o], y_at, c), wc_send.at[o, y_flip], wc_recv.at[o, y_flip], core_dev)
+
+    def from_line(o):
+        if o:
+            arrive(columns(there[o], y, c), pz_send.at[o], pz_recv.at[o])
+            arrive(share(there[o], y, c), wz_send.at[o], wz_recv.at[o])
+        pass_on(o, 0)
+
+    def from_y(o):
+        arrive(columns(there[o], 1 - y, c), py_send.at[o], py_recv.at[o])
+        arrive(share(there[o], 1 - y, c), wy_send.at[o], wy_recv.at[o])
+        pass_on(o, 1)
+
+    def from_core(o):
+        for y_flip in range(2):
+            y_at = 1 - y if y_flip else y
+            arrive(columns(there[o], y_at, 1 - c), pc_send.at[o, y_flip], pc_recv.at[o, y_flip])
+            arrive(share(there[o], y_at, 1 - c), wc_send.at[o, y_flip], wc_recv.at[o, y_flip])
+
+    lane = lax.broadcasted_iota(jnp.int32, (rows, 128), 1)
+    query_pos = lax.broadcasted_iota(jnp.int32, (rows, 2 * rows), 0) + rows
+    key_pos = lax.broadcasted_iota(jnp.int32, (rows, 2 * rows), 1)
+    inside = (
+        (key_pos <= query_pos)
+        & (key_pos > query_pos - WINDOW_KEYS)
+        & (key_pos + ctx * rows >= rows)
+    )
+
+    def attention(group):
+        key_value = keys[:, group * 128 : group * 128 + 128]
+        value_key = keys[:, 256 + group * 128 : 256 + group * 128 + 128]
+
+        @pl.loop(0, 4)
+        def _(step):
+            pair = group * 4 + step
+            cols = pl.ds(pl.multiple_of(pair * 128, 128), 128)
+            both = q_ref[:, cols]
+            mixed = []
+            for odd in range(2):
+                q = jnp.where((lane >= 64) if odd else (lane < 64), both, jnp.zeros_like(both))
+                sink = sink_ref[pair * 2 + odd]
+                score = lax.dot_general(
+                    q, value_key if odd else key_value, (((1,), (1,)), ((), ())),
+                    preferred_element_type=jnp.float32,
+                ) * 0.125
+                top = jnp.maximum(jnp.max(jnp.where(inside, score, -1e30), -1, keepdims=True), sink)
+                vals = jnp.where(inside, jnp.exp(score - top), 0.0)
+                under = jnp.sum(vals, -1, keepdims=True) + jnp.exp(sink - top)
+                probs = (vals / under).astype(jnp.bfloat16)
+                mixed.append(
+                    jnp.dot(probs, key_value if odd else value_key, preferred_element_type=jnp.float32)
+                )
+            att[:, cols] = jnp.where(lane < 64, mixed[0], mixed[1]).astype(jnp.bfloat16)
+
+    span = 4 * wide
+
+    def project(o):
+        near = pl.ds(pl.multiple_of(there[o] * span, 16), span)
+        value = lax.dot_general(
+            att[...], proj[near], (((1,), (1,)), ((), ())), preferred_element_type=jnp.float32
+        )
+        sums[there[o]] = value
+        outgoing[there[o]] = value.astype(jnp.bfloat16)
+        slot = there[o] % 2
+
+        @pl.when(there[o] // 2 != x)
+        def _():
+            remote(
+                outgoing.at[there[o]], incoming.at[slot], x_send.at[slot], x_recv.at[slot], x_dev
+            ).start()
+
+    from_line(0)
+    for keep in keeps:
+        keep.wait()
+    arrive(keys.at[pl.ds(0, rows)], kv_send.at[0], kv_recv.at[0])
+    attention(0)
+    from_line(1)
+    from_y(0)
+    attention(1)
+    from_line(2)
+    from_y(1)
+    from_core(0)
+    project(0)
+    from_line(3)
+    from_y(2)
+    from_core(1)
+    project(1)
+    from_y(3)
+    from_core(2)
+    project(2)
+    from_core(3)
+    project(3)
+    squares = jnp.zeros((rows, 1), jnp.float32)
+    for slot in range(2):
+        arrive(incoming.at[slot], x_send.at[slot], x_recv.at[slot])
+        cols = pl.ds(slot * span, span)
+        value = (
+            hidden_ref[:, cols].astype(jnp.float32)
+            + (sums[2 * x + slot] + incoming[slot].astype(jnp.float32))
+        )
+        residual_ref[:, cols] = value
+        squares = squares + jnp.sum(value * value, -1, keepdims=True)
+    square_out[...] = jnp.broadcast_to(squares, square_out.shape)
+    send(square_out, square_in, s_send.at[0], s_recv.at[0], x_dev)
+    arrive(square_in, s_send.at[0], s_recv.at[0])
+    total = squares + square_in[:, 0:1]
+    scale = lax.rsqrt(total / (2 * residual_ref.shape[1]) + 1e-05)
+    normed_ref[...] = (residual_ref[...] * scale * gain_ref[...]).astype(jnp.bfloat16)
+    for slot in range(2):
+        remote(
+            outgoing.at[2 * (1 - x) + slot], incoming.at[slot], x_send.at[slot], x_recv.at[slot], x_dev
+        ).wait_send()
+    for copy in sends:
+        copy.wait_send()
+
+
+def dense_layer(
+    hidden_in, queries, rotated_key_value, sink_logit_table, out_proj, norm_gain,
+    expert_in, expert_out, routes, route_scores,
+):
+    rows, width = hidden_in.shape
+    heads_width = queries.shape[1]
+    experts = lax.axis_size("ctx")
+    weights = route_scores / jnp.sum(route_scores, -1, keepdims=True)
+    chosen = routes[:, :, None] == jnp.arange(experts, dtype=jnp.int32)
+    spread = jnp.sum(jnp.where(chosen, weights[:, :, None], 0.0), 1).T
+    key_value = rotated_key_value.reshape(rows, -1)
+    value_key = jnp.concatenate([rotated_key_value[..., 64:], rotated_key_value[..., :64]], -1)
+    pairs = jnp.concatenate([key_value, value_key.reshape(rows, -1)], 1)
+    wide = out_proj.shape[1]
+    dma = pltpu.SemaphoreType.DMA
+    bf16, f32 = jnp.bfloat16, jnp.float32
+    vmem = pl.BlockSpec(memory_space=pltpu.VMEM)
+    residual, normed, table = pl.pallas_call(
+        front_kernel,
+        out_shape=(
+            jax.ShapeDtypeStruct((rows, width), f32),
+            jax.ShapeDtypeStruct((rows, width), bf16),
+            jax.ShapeDtypeStruct((experts, experts, rows), f32),
+        ),
+        in_specs=[vmem, vmem, pl.BlockSpec(memory_space=pltpu.SMEM)] + [vmem] * 4,
+        out_specs=(vmem, vmem, vmem),
+        scratch_shapes=[
+            pltpu.VMEM((2 * rows, 512), bf16),
+            pltpu.VMEM((experts * wide, heads_width), bf16),
+            pltpu.VMEM((rows, heads_width), bf16),
+            pltpu.VMEM((4, rows, 4 * wide), f32),
+            pltpu.VMEM((4, rows, 4 * wide), bf16),
+            pltpu.VMEM((2, rows, 4 * wide), bf16),
+            pltpu.VMEM((rows, 128), f32),
+            pltpu.VMEM((rows, 128), f32),
+            dma((3,)), dma((1,)), dma((1,)), dma((2,)), dma((2,)), dma((1,)), dma((1,)),
+        ]
+        + ([dma((4,))] * 4 + [dma((4, 2))] * 2) * 2,
+        compiler_params=pltpu.CompilerParams(
+            collective_id=2, has_side_effects=True, vmem_limit_bytes=32 * 2**20
+        ),
+        cost_estimate=pl.CostEstimate(flops=10**9, bytes_accessed=4 * 2**20, transcendentals=0),
+    )(queries, pairs, sink_logit_table, out_proj.T, spread, hidden_in, norm_gain[None, :])
+    mine = lax.dynamic_slice_in_dim(table, lax.axis_index("ctx"), 1, 1).reshape(experts * rows, 1)
+    return dense_experts(residual, normed, expert_in, expert_out, mine)
+
+
+def dense_experts(residual, normed, expert_in, expert_out, mine):
     experts = lax.axis_size("ctx")
     rows, width = normed.shape
-    chosen = routes[:, :, None] == jnp.arange(experts, dtype=jnp.int32)
-    spread = jnp.sum(jnp.where(chosen, weights[:, :, None], 0.0), 1)
-    every = lax.all_gather(spread, "ctx", axis=0, tiled=True)
-    mine = lax.dynamic_slice_in_dim(every, lax.axis_index("ctx"), 1, 1)
     dma = pltpu.SemaphoreType.DMA
     bf16 = jnp.bfloat16
     vmem = pl.BlockSpec(memory_space=pltpu.VMEM)
@@ -317,6 +547,12 @@
     route_scores,
 ):
     tok_rows = hidden_in.shape[0]
+    small = lax.axis_size("ctx") == 16 and lax.axis_size("tp") == 2
+    if small and rotated_key_value.shape[1:] == (2, 128) and tok_rows == 128:
+        return dense_layer(
+            hidden_in, queries, rotated_key_value, sink_logit_table, out_proj, norm_gain,
+            expert_in, expert_out, routes, route_scores,
+        )
     kv_heads = rotated_key_value.shape[1]
     head_dim = rotated_key_value.shape[2] // 2
     q_heads = sink_logit_table.shape[0]
@@ -360,8 +596,6 @@
     )
     ctx_count = lax.axis_size("ctx")
     weights = route_scores / jnp.sum(route_scores, -1, keepdims=True)
-    if ctx_count == 16 and lax.axis_size("tp") == 2 and expert_in.shape[0] == 1:
-        return dense_experts(residual, normed, expert_in, expert_out, routes, weights)
     tp_count = lax.axis_size("tp")
     top_count = routes.shape[1]
     experts = ctx_count * expert_in.shape[0]

time: 209 us -> 167 us (0.80)
  Pallas kernels: 109 us -> 156 us
  waiting for transfers between devices: 43.9 us -> 0 us
  blocking collectives: 27.1 us -> 0 us
  between operations: 13.5 us -> 0.07 us
  matrix products: 4.95 us -> 0 us
  local copies, waits for them, and re-layouts: 3.95 us -> 7.12 us
  starting transfers between devices: 2.4 us -> 0 us
    pallas_call x0 -> x1, Pallas kernels: none -> 47.6 us  [dense_layer(): pl.pallas_call(front_kernel, out_shape=(jax.ShapeDtypeStruct((rows, width...]
    all_gather x1 -> x0, waiting for transfers between devices: 43.1 us -> none  [body(): lax.all_gather(out_proj, 'ctx', axis=1, tiled=True)]
    all_gather x1 -> x0, blocking collectives: 22.2 us -> none  [dense_experts(): every = lax.all_gather(spread, 'ctx', axis=0, tiled=True)]
    dot_general x3 -> x0, matrix products: 4.95 us -> none  [the longest x1 3.83 us: body(): jnp.dot(outputs, lax.all_gather(out_proj, 'ctx', axis=1, tiled=True), pre...]
    psum x1 -> x0, blocking collectives: 4.93 us -> none  [body(): square_total = lax.psum(jnp.sum(residual * residual, -1), 'tp')]
    ppermute x1 -> x0, starting transfers between devices: 2.36 us -> none  [shifted(): lax.ppermute(value, axis, [(source, source + steps) for source in range(f...]
  transfers between devices with their start and end apart: 3 -> 0, of which waited for: 1 -> 0; matrix products, arithmetic and copies ran while one was open for 2% -> 0% of each run, Pallas kernels for 0% -> 0%
where the time goes in v3:
time: 167 us; the launch traced here: 165 us
  Pallas kernels  156 us (93%)
  local copies, waits for them, and re-layouts  7.12 us (4%)
  other arithmetic  2.27 us (1%)
    pallas_call x1, Pallas kernels, dense_experts(): pl.pallas_call(expert_kernel, out_shape=jax.ShapeDtypeStruct((rows, width...  108 us
    pallas_call x1, Pallas kernels, dense_layer(): pl.pallas_call(front_kernel, out_shape=(jax.ShapeDtypeStruct((rows, width...  47.6 us
    unnamed x9, local copies, waits for them, and re-layouts  4.13 us

profile of v3, /device:TPU:0, one launch (start us, length us, event | category | flops | bytes accessed | tf_op | source)
XLA Modules:
  0.0 165.4 jit_solution(16866806527281557515)
XLA Ops:
  0.0 0.7 reduce_sum.18
  0.7 0.7 broadcast_divide_fusion
  1.4 0.7 broadcast_in_dim.21.gain_ref
  2.1 0.7 select_reduce_fusion
  2.8 1.1 fusion
  3.8 0.2 pad_maximum_fusion.1
  4.0 0.9 copy_bitcast_fusion
  4.9 0.0 copy-start
  4.9 0.9 copy-done
  5.9 0.0 copy-start.1
  5.9 0.9 copy-done.1
  6.8 0.0 copy-start.2
  6.8 0.9 copy-done.2
  7.7 0.0 copy-start.3
  7.7 0.7 copy-done.3
  8.4 47.6 %shard_map.100 = (f32[128,768]{1,0:T(8,128)S(1)}, bf16[128,768]{1,0:T(8,128)(2,1)S(1)}, f32[16,16,128]{2,1,0:T(8,128)S(1)}) custom-call(bf16[128,1024]{1,0:T(8,128)(2,1)S(1)} %copy-done, bf16[128,512]{1,0:T(8,128)(2,1)S(1)} %pad_maximum_fusion.kv_ref, f32[16]{0:T(128)S(1)} %copy-done.3, bf16[96,1024]{1,0:T(8,128)(2,1)S(1)} %bitcast.13, ...), custom_call_target="tpu_custom_call" | custom-call | flops 1000000000 | bytes 4194304 | tf_op jit(solution)/shard_map/pallas_call | solution.py:466
  56.0 0.4 copy.16.mine_ref
  56.4 108.3 %shard_map.101 = bf16[128,768]{1,0:T(8,128)(2,1)S(1)} custom-call(bf16[128,768]{1,0:T(8,128)(2,1)S(1)} %get-tuple-element.8.normed_ref, f32[2048,1]{1,0:T(8,128)S(1)} %copy.16.mine_ref, f32[128,768]{1,0:T(8,128)S(1)} %get-tuple-element.10.residual_ref, bf16[2,1536,768]{2,1,0:T(8,128)(2,1)} %bitcast.16, bf16[768,1536]{1,0:T(8,128)(2,1)} %bitcast.17), custom_call_target="tpu_custom_call" | custom-call | flops 14495514624 | bytes 8388608 | tf_op jit(solution)/shard_map/pallas_call | solution.py:505
  164.7 0.7 copy.22
  (2 shorter events, 0.0 us)
Async XLA Ops:
  4.9 1.0 copy-start
  5.9 0.9 copy-start.1
  6.8 0.9 copy-start.2
  7.7 0.7 copy-start.3

commit v4 on v3

--- a/solution.py
+++ b/solution.py
@@ -88,12 +88,13 @@
 
     own = normed_ref
     own_copies = []
+    for o in (1, 2, 3):
+        for chunk in range(2):
+            src = own.at[pl.ds(chunk * half, half)]
+            dst = piece(chunk, 0, 0, 0, 0)
+            send(src, dst, gz_send.at[chunk, o], gz_recv.at[chunk, o], z_devs[o])
     for chunk in range(2):
-        src = own.at[pl.ds(chunk * half, half)]
-        dst = piece(chunk, 0, 0, 0, 0)
-        for o in (3, 2, 1):
-            send(src, dst, gz_send.at[chunk, o], gz_recv.at[chunk, o], z_devs[o])
-        keep = pltpu.make_async_copy(src, dst, own_sem.at[chunk])
+        keep = pltpu.make_async_copy(own.at[pl.ds(chunk * half, half)], piece(chunk, 0, 0, 0, 0), own_sem.at[chunk])
         keep.start()
         own_copies.append(keep)
 
@@ -109,14 +110,18 @@
     def arrive(dst, s_sem, r_sem):
         remote(dst, dst, s_sem, r_sem, core_dev).wait_recv()
 
-    def gather(o):
+    def line(o):
         for chunk in range(2):
             if o:
                 arrive(piece(chunk, o, 0, 0, 0), gz_send.at[chunk, o], gz_recv.at[chunk, o])
             pass_on(chunk, o, 0, 0)
+
+    def via_first(o):
         for chunk in range(2):
             arrive(piece(chunk, o, 1, 0, 0), g1_send.at[chunk, o], g1_recv.at[chunk, o])
             pass_on(chunk, o, 1, 0)
+
+    def via_second(o):
         for one in range(2):
             for chunk in range(2):
                 arrive(piece(chunk, o, one, 1, 0), g2_send.at[chunk, o, one], g2_recv.at[chunk, o, one])
@@ -220,28 +225,36 @@
                     rz_send.at[o, chunk], rz_recv.at[o, chunk], z_devs[o],
                 )
 
-    gather(0)
+    line(0)
+    via_first(0)
+    line(1)
+    via_second(0)
+    via_first(1)
+    line(2)
+    via_second(1)
+    via_first(2)
+    line(3)
     for keep in own_copies:
         keep.wait()
     for load in loads:
         load.wait()
     gather_core(0)
     compute(0)
-    gather(1)
+    via_first(3)
+    via_second(2)
     gather_core(1)
     compute(1)
     reduce_core(0)
-    gather(2)
+    via_second(3)
     gather_core(2)
     compute(2)
+    reduce_two(0)
     reduce_core(1)
-    reduce_two(0)
-    gather(3)
     gather_core(3)
     compute(3)
+    reduce_one(0)
     reduce_core(2)
     reduce_two(1)
-    reduce_one(0)
     reduce_core(3)
     reduce_two(2)
     reduce_one(1)
@@ -310,7 +323,7 @@
         remote(dst, dst, s_sem, r_sem, core_dev).wait_recv()
 
     send(kv_ref, keys.at[pl.ds(0, rows)], kv_send.at[0], kv_recv.at[0], next_dev)
-    for o in (3, 2, 1):
+    for o in (1, 2, 3):
         send(proj_ref, columns(z, y, c), pz_send.at[o], pz_recv.at[o], z_devs[o])
         send(spread_ref, share(z, y, c), wz_send.at[o], wz_recv.at[o], z_devs[o])
     keeps = [
@@ -408,12 +421,12 @@
     attention(0)
     from_line(1)
     from_y(0)
-    attention(1)
     from_line(2)
     from_y(1)
+    attention(1)
+    from_line(3)
     from_core(0)
     project(0)
-    from_line(3)
     from_y(2)
     from_core(1)
     project(1)
@@ -453,9 +466,8 @@
     rows, width = hidden_in.shape
     heads_width = queries.shape[1]
     experts = lax.axis_size("ctx")
-    weights = route_scores / jnp.sum(route_scores, -1, keepdims=True)
     chosen = routes[:, :, None] == jnp.arange(experts, dtype=jnp.int32)
-    spread = jnp.sum(jnp.where(chosen, weights[:, :, None], 0.0), 1).T
+    spread = jnp.sum(jnp.where(chosen, route_scores[:, :, None], 0.0), 1).T
     key_value = rotated_key_value.reshape(rows, -1)
     value_key = jnp.concatenate([rotated_key_value[..., 64:], rotated_key_value[..., :64]], -1)
     pairs = jnp.concatenate([key_value, value_key.reshape(rows, -1)], 1)
@@ -489,7 +501,8 @@
         ),
         cost_estimate=pl.CostEstimate(flops=10**9, bytes_accessed=4 * 2**20, transcendentals=0),
     )(queries, pairs, sink_logit_table, out_proj.T, spread, hidden_in, norm_gain[None, :])
-    mine = lax.dynamic_slice_in_dim(table, lax.axis_index("ctx"), 1, 1).reshape(experts * rows, 1)
+    mine = lax.dynamic_slice_in_dim(table, lax.axis_index("ctx"), 1, 1)
+    mine = (mine / jnp.sum(table, 1, keepdims=True)).reshape(experts * rows, 1)
     return dense_experts(residual, normed, expert_in, expert_out, mine)
 
 

time: 167 us -> 126 us (0.75)
  Pallas kernels: 156 us -> 117 us
    pallas_call x1, Pallas kernels: 108 us -> 74.4 us  [dense_experts(): pl.pallas_call(expert_kernel, out_shape=jax.ShapeDtypeStruct((rows, width...]
    pallas_call x1, Pallas kernels: 47.6 us -> 42.6 us  [dense_layer(): pl.pallas_call(front_kernel, out_shape=(jax.ShapeDtypeStruct((rows, width...]
where the time goes in v4:
time: 126 us; the launch traced here: 125 us
  Pallas kernels  117 us (93%)
  local copies, waits for them, and re-layouts  7.1 us (6%)
    pallas_call x1, Pallas kernels, dense_experts(): pl.pallas_call(expert_kernel, out_shape=jax.ShapeDtypeStruct((rows, width...  74.4 us
    pallas_call x1, Pallas kernels, dense_layer(): pl.pallas_call(front_kernel, out_shape=(jax.ShapeDtypeStruct((rows, width...  42.6 us
    unnamed x9, local copies, waits for them, and re-layouts  4.13 us

profile of v4, /device:TPU:0, one launch (start us, length us, event | category | flops | bytes accessed | tf_op | source)
XLA Modules:
  0.0 125.1 jit_solution(4265348156584460343)
XLA Ops:
  0.0 0.7 broadcast_in_dim.23.gain_ref
  0.7 0.7 select_reduce_fusion
  1.4 1.1 fusion.1
  2.5 0.2 pad_maximum_fusion.1
  2.6 0.9 copy_bitcast_fusion
  3.5 0.0 copy-start
  3.5 0.9 copy-done
  4.5 0.0 copy-start.1
  4.5 0.9 copy-done.1
  5.4 0.0 copy-start.2
  5.4 0.9 copy-done.2
  6.3 0.0 copy-start.3
  6.3 0.7 copy-done.3
  7.0 42.6 %shard_map.100 = (f32[128,768]{1,0:T(8,128)S(1)}, bf16[128,768]{1,0:T(8,128)(2,1)S(1)}, f32[16,16,128]{2,1,0:T(8,128)S(1)}) custom-call(bf16[128,1024]{1,0:T(8,128)(2,1)S(1)} %copy-done, bf16[128,512]{1,0:T(8,128)(2,1)S(1)} %pad_maximum_fusion.kv_ref, f32[16]{0:T(128)S(1)} %copy-done.3, bf16[96,1024]{1,0:T(8,128)(2,1)S(1)} %bitcast.14, ...), custom_call_target="tpu_custom_call" | custom-call | flops 1000000000 | bytes 4194304 | tf_op jit(solution)/shard_map/pallas_call | solution.py:478
  49.6 0.4 copy.16.mine_ref
  50.0 74.4 %shard_map.101 = bf16[128,768]{1,0:T(8,128)(2,1)S(1)} custom-call(bf16[128,768]{1,0:T(8,128)(2,1)S(1)} %get-tuple-element.8.normed_ref, f32[2048,1]{1,0:T(8,128)S(1)} %copy.16.mine_ref, f32[128,768]{1,0:T(8,128)S(1)} %get-tuple-element.10.residual_ref, bf16[2,1536,768]{2,1,0:T(8,128)(2,1)} %bitcast.18, bf16[768,1536]{1,0:T(8,128)(2,1)} %bitcast.19), custom_call_target="tpu_custom_call" | custom-call | flops 14495514624 | bytes 8388608 | tf_op jit(solution)/shard_map/pallas_call | solution.py:518
  124.4 0.7 copy.22
  (3 shorter events, 0.1 us)
Async XLA Ops:
  3.5 1.0 copy-start
  4.5 0.9 copy-start.1
  5.4 0.9 copy-start.2
  6.3 0.7 copy-start.3
